TPU v7x, 1024 devices: a whole 8x8x8 slice. The times are simulated.
1024 devices in a mesh: rep: 16 (over x, core), exp: 64 (over y, z).
Axes of the slice: x: 8, y: 8, z: 8, core: 2. Of those that a mesh axis runs over, the one named last changes fastest.
Arguments:
- prompt_state: bfloat16 [512, 16, 128, 128], P('exp', 'rep'), may hold values from -6 to 6
- prompt_conv: bfloat16 [512, 16, 3, 384], P('exp', 'rep'), may hold values from -6 to 6
- slot_prompt: int32 [8192], P(('rep', 'exp')), may hold values from 0 to 7, as said below
- projected: bfloat16 [8192, 4, 16, 384], P(('rep', 'exp')), may hold values from -6 to 6
- conv_weight: bfloat16 [16, 4, 384], replicated, may hold values from -3 to 3
- log_decay: float32 [8192, 4, 16], P(('rep', 'exp')), may hold values from -2.5 to -0.02
- write_rate: float32 [8192, 4, 16], P(('rep', 'exp')), may hold values from 0.05 to 0.95
- gate_in: bfloat16 [8192, 4, 2048], P(('rep', 'exp')), may hold values from -6 to 6
- layer_in: bfloat16 [8192, 4, 2048], P(('rep', 'exp')), may hold values from -3 to 3
- head_gain: float32 [128], replicated, may hold values from 0.1 to 1.9
- post_gain: float32 [2048], replicated, may hold values from 0.1 to 1.9
- expert_ids: int32 [8192, 4, 10], P(('rep', 'exp')), may hold values from 0 to 63, all different within a row; in each aligned block of 32 rows (0 to 31, 32 to 63, ..., all dimensions but the last counted through in order) at most 8 rows name the same one
- route_weight: float32 [8192, 4, 10], P(('rep', 'exp')), may hold values from 0.02 to 0.25
- w_gate_up: bfloat16 [64, 2048, 1024], P('exp'), may hold values from -0.125 to 0.125
- w_down: bfloat16 [64, 512, 2048], P('exp'), may hold values from -0.25 to 0.25
Outputs:
- layer_out: bfloat16 [8192, 4, 2048], P(('rep', 'exp'))
Inputs may be any that keep to these rules, and one draw needn't show every extreme that they name: `slot_prompt`: in every sample group (the devices that share an index along exp) each of the group's 8 prompts is named by exactly 16 of the group's samples. `expert_ids`: the 32 rows of one device name no expert more than 8 times, a bound that some block reaches; a row names 10 different experts.
All inputs are finite; a program needn't handle non-finite values.
Results may differ from a plain program's by a relative error of at most 0.012.
Values may be sent and summed in bfloat16 or wider, within the bound.
A program may use at most 32 MiB of HBM per device.

v0:
```python
import jax
import jax.numpy as jnp
from jax import lax
from jax.sharding import PartitionSpec as P

DK = 128
CONV = 4
FE = 512
STEPS = 4


EPSILON = 1e-06
HIGHEST = lax.Precision.HIGHEST


def swish(inputs):
    return inputs * jax.nn.sigmoid(inputs)


def conv_features(projected, conv_window, conv_weight):
    history = jnp.concatenate([jnp.transpose(conv_window, (0, 2, 1, 3)), projected], axis=1).astype(
        jnp.float32
    )
    taps_all = conv_weight.astype(jnp.float32)
    summed = jnp.zeros(projected.shape, jnp.float32)
    for tap_index in range(CONV):
        summed = summed + history[:, tap_index : tap_index + STEPS] * taps_all[:, tap_index]
    active = swish(summed)
    queries = active[..., :DK]
    keys_part = active[..., DK : 2 * DK]
    values_part = active[..., 2 * DK :]
    queries = (
        queries
        / jnp.sqrt(jnp.sum(queries * queries, axis=-1, keepdims=True) + EPSILON)
        * DK ** (-0.5)
    )
    keys_part = keys_part / jnp.sqrt(
        jnp.sum(keys_part * keys_part, axis=-1, keepdims=True) + EPSILON
    )
    return (
        queries.astype(jnp.bfloat16),
        keys_part.astype(jnp.bfloat16),
        values_part.astype(jnp.bfloat16),
    )


def mix_heads(read_all, gate_in, layer_in, head_gain, post_gain):
    normed = (
        read_all
        / jnp.sqrt(jnp.mean(read_all * read_all, axis=-1, keepdims=True) + EPSILON)
        * head_gain
    )
    flat_heads = normed.reshape(normed.shape[0], normed.shape[1], -1)
    residual = layer_in.astype(jnp.float32) + flat_heads * swish(gate_in.astype(jnp.float32))
    scaled = (
        residual
        / jnp.sqrt(jnp.mean(residual * residual, axis=-1, keepdims=True) + EPSILON)
        * post_gain
    )
    return (residual, scaled.astype(jnp.bfloat16))


def per_device(
    prompt_state,
    prompt_conv,
    slot_prompt,
    projected,
    conv_weight,
    log_decay,
    write_rate,
    gate_in,
    layer_in,
    head_gain,
    post_gain,
    expert_ids,
    route_weight,
    w_gate_up,
    w_down,
):
    samples_n = projected.shape[0]
    prompts_n = prompt_state.shape[0]
    prompt_ids = jnp.arange(prompts_n, dtype=jnp.int32)
    picker = (slot_prompt[:, None] == prompt_ids[None, :]).astype(jnp.bfloat16)
    states_all, conv_all = (
        lax.all_gather(prompt_state, "rep", axis=1, tiled=True),
        lax.all_gather(prompt_conv, "rep", axis=1, tiled=True),
    )
    conv_mine = jnp.einsum(
        "sp,phcw->shcw", picker, conv_all, preferred_element_type=jnp.float32
    ).astype(jnp.bfloat16)
    queries, keys_part, values_part = conv_features(projected, conv_mine, conv_weight)
    vectors = jnp.concatenate([queries, keys_part], axis=1)
    start_state = jnp.einsum(
        "sp,phde->shde", picker, states_all, preferred_element_type=jnp.float32
    ).astype(jnp.bfloat16)
    projections = jnp.einsum(
        "smhd,shde->smhe", vectors, start_state, preferred_element_type=jnp.float32
    )
    proj_queries = projections[:, :STEPS]
    proj_keys = projections[:, STEPS:]
    queries_f = queries.astype(jnp.float32)
    keys_f = keys_part.astype(jnp.float32)
    values_f = values_part.astype(jnp.float32)
    cumulative = jnp.cumsum(log_decay, axis=1)
    writes_list = []
    reads_list = []
    for position in range(STEPS):
        decay_now = jnp.exp(cumulative[:, position])[:, :, None]
        recalled = decay_now * proj_keys[:, position]
        for earlier_pos in range(position):
            ratio_now = jnp.exp(cumulative[:, position] - cumulative[:, earlier_pos])[:, :, None]
            intersection = jnp.sum(
                keys_f[:, earlier_pos] * keys_f[:, position], axis=-1, keepdims=True
            )
            recalled = recalled + ratio_now * intersection * writes_list[earlier_pos]
        written = write_rate[:, position][:, :, None] * (values_f[:, position] - recalled)
        writes_list.append(written)
        reading = decay_now * proj_queries[:, position]
        for earlier_pos in range(position + 1):
            ratio_now = jnp.exp(cumulative[:, position] - cumulative[:, earlier_pos])[:, :, None]
            intersection = jnp.sum(
                keys_f[:, earlier_pos] * queries_f[:, position], axis=-1, keepdims=True
            )
            reading = reading + ratio_now * intersection * writes_list[earlier_pos]
        reads_list.append(reading)
    read_all = jnp.stack(reads_list, axis=1)
    residual, normed_in = mix_heads(read_all, gate_in, layer_in, head_gain, post_gain)
    rows_n = samples_n * STEPS
    topk_n = expert_ids.shape[2]
    experts_n = lax.axis_size("exp") * w_gate_up.shape[0]
    cap_slots = max(2, (rows_n * topk_n * 8 + experts_n * 5 - 1) // (experts_n * 5))
    chosen = expert_ids.reshape(-1)
    entries_n = chosen.shape[0]
    entry_order = jnp.arange(entries_n, dtype=jnp.int32)
    earlier = (chosen[:, None] == chosen[None, :]) & (entry_order[None, :] < entry_order[:, None])
    slot_index = jnp.sum(earlier.astype(jnp.int32), axis=1)
    target = chosen * cap_slots + slot_index
    placing = (
        target[:, None] == jnp.arange(experts_n * cap_slots, dtype=jnp.int32)[None, :]
    ).astype(jnp.float32)
    sources = (
        (entry_order // topk_n)[:, None] == jnp.arange(rows_n, dtype=jnp.int32)[None, :]
    ).astype(jnp.float32)
    dispatch = jnp.einsum("ec,er->cr", placing, sources, precision=HIGHEST).astype(jnp.bfloat16)
    flat_rows = normed_in.reshape(rows_n, -1)
    buffer_out = jnp.dot(dispatch, flat_rows, preferred_element_type=jnp.float32).astype(
        jnp.bfloat16
    )
    buffer_out = buffer_out.reshape(experts_n, cap_slots, flat_rows.shape[1])
    arrived = lax.all_to_all(buffer_out, "exp", split_axis=0, concat_axis=0, tiled=True)
    flat_in = arrived.reshape(-1, arrived.shape[-1])
    both_parts = jnp.dot(flat_in, w_gate_up[0], preferred_element_type=jnp.float32)
    hidden = (swish(both_parts[:, :FE]) * both_parts[:, FE:]).astype(jnp.bfloat16)
    expert_out = jnp.dot(hidden, w_down[0], preferred_element_type=jnp.float32).astype(jnp.bfloat16)
    returned = lax.all_to_all(
        expert_out.reshape(arrived.shape), "exp", split_axis=0, concat_axis=0, tiled=True
    )
    weighting = jnp.einsum(
        "er,ec->rc", sources, placing * route_weight.reshape(-1)[:, None], precision=HIGHEST
    )
    gathered_out = returned.reshape(experts_n * cap_slots, -1).astype(jnp.float32)
    routed = jnp.dot(weighting, gathered_out, precision=HIGHEST)
    result = residual.reshape(rows_n, -1) + routed
    return result.reshape(layer_in.shape).astype(jnp.bfloat16)


def solution(mesh):
    in_specs = (
        P("exp", "rep", None, None),
        P("exp", "rep", None, None),
        P(("rep", "exp")),
        P(("rep", "exp"), None, None, None),
        P(),
        P(("rep", "exp"), None, None),
        P(("rep", "exp"), None, None),
        P(("rep", "exp"), None, None),
        P(("rep", "exp"), None, None),
        P(),
        P(),
        P(("rep", "exp"), None, None),
        P(("rep", "exp"), None, None),
        P("exp", None, None),
        P("exp", None, None),
    )
    out_specs = P(("rep", "exp"), None, None)
    return jax.shard_map(
        per_device, mesh=mesh, in_specs=in_specs, out_specs=out_specs, check_vma=False
    )
```

profile of v0, /device:TPU:48, one launch (start us, length us, event | category | flops | bytes accessed | tf_op | source)
XLA Modules:
  0.0 232.2 jit_solution(3651416413631196776)
XLA Ops:
  6.5 0.7 all-gather.2.cloned.1.call-update
  7.3 0.8 reshape.338
  8.1 18.0 %all_gather.7 = bf16[8,16,3,384]{3,0,2,1:T(8,128)(2,1)S(1)} all-gather(bf16[8,1,3,384]{3,0,2,1:T(8,128)(2,1)} %param.16), channel_id=1, replica_groups=mesh['rep'=16,'exp'=64] {'rep'}, dimensions={1}, use_global_device_ids=true | all-gather | bytes 313344 | tf_op jit(solution)/shard_map/all_gather | solution.py:86
  26.1 0.9 fusion.18
  27.1 0.2 copy.109
  27.3 0.2 copy.110
  27.4 0.4 maximum_convert_fusion
  27.9 0.9 divide_multiply_fusion
  28.8 0.3 multiply_reduce_fusion.2
  29.7 0.2 convert_reduce_fusion
  30.0 0.3 fusion.78
  30.4 4.3 %multiply_reduce_fusion.17 = (f32[8,16]{1,0:T(8,128)S(1)}, f32[8,16]{1,0:T(8,128)S(1)}, f32[8,16]{1,0:T(8,128)S(1)}, f32[8,16]{1,0:T(8,128)S(1)}, f32[8,16]{1,0:...) fusion(f32[8,4,16,128]{3,1,2,0:T(4,128)S(1)} %get-tuple-element, ...), kind=kLoop, calls=%fused_computation.108 | loop fusion | flops 522240 | bytes 532480 | tf_op jit(solution)/shard_map/reduce_sum | solution.py:121
  34.7 0.3 convolution_convert_fusion.3
  35.2 33.1 %all-gather.2.cloned.1.call-done = bf16[8,16,128,128]{3,2,0,1:T(8,128)(2,1)} async-done(((bf16[8,1,128,128]{3,2,0,1:T(8,128)(2,1)}), bf16[8,16,128,128]{3,2,0,1:T(8,128)(2,1)}) %all-gather.2.cloned.1.call-update) | async-done | bytes 4194320 | tf_op jit(solution)/shard_map/all_gather | solution.py:85
  68.2 4.7 %fusion.8 = bf16[8,16,128,128]{3,0,2,1:T(8,128)(2,1)S(1)} fusion(bf16[8,16,128,128]{3,2,0,1:T(8,128)(2,1)} %all-gather.2.cloned.1.call-done, s32[8]{0:T(128)S(1)} %copy-done.13), kind=kOutput, calls=%fused_computation.10 | convolution fusion | flops 35651648 | bytes 8388640 | tf_op jit(solution)/shard_map/sp,phde->shde/dot_general | solution.py:93
  73.0 1.2 fusion.15
  74.2 0.5 fusion.58
  74.7 1.0 fusion.56
  75.8 1.7 multiply_add_fusion.1
  77.5 2.5 %multiply_add_fusion = f32[8,1,16,128]{3,1,2,0:T(1,128)S(1)} fusion(f32[8,8,16,128]{3,1,2,0:T(8,128)S(1)} %fusion.15, f32[8,1,16,128]{3,1,2,0:T(1,128)S(1)} %get-tuple-element.26, f32[8,4,16,128]{3,1,2,0:T(4,128)S(1)} %fusion.40, f32[8,16]{1,0:T(8,128)S(1)} %get-tuple-element.47, f32[8,16]{1,0:T(8,128)S(1)} %get-tuple-element.48, ...), kind=kLoop, calls=%fused_computation.92 | loop fusion | flops 491520 | bytes 598016 | tf_op jit(solution)/shard_map/add | solution.py:124
  80.0 0.3 fusion.39
  80.8 0.6 multiply_reduce_fusion
  81.4 0.1 multiply_convert_fusion
  81.6 0.7 fusion.6
  82.3 69.4 %all_to_all.10 = bf16[64,8,2048]{2,1,0:T(8,128)(2,1)S(1)} all-to-all(bf16[64,8,2048]{2,1,0:T(8,128)(2,1)S(1)} %fusion.6), channel_id=1, replica_groups=mesh['rep'=16,'exp'=64] {'exp'}, dimensions={0} | all-to-all | bytes 4194304 | tf_op jit(solution)/shard_map/all_to_all | solution.py:150
  151.8 2.3 %fusion = f32[512,1024]{1,0:T(8,128)S(1)} fusion(bf16[1,2048,1024]{2,1,0:T(8,128)(2,1)S(1)} %copy-done.15, bf16[64,8,2048]{2,1,0:T(8,128)(2,1)S(1)} %all_to_all.10), kind=kOutput, calls=%fused_computation | convolution fusion | flops 2147483648 | bytes 8388608 | tf_op jit(solution)/shard_map/dot_general | solution.py:152
  154.1 2.6 %fusion.7 = bf16[64,8,2048]{2,1,0:T(8,128)(2,1)} fusion(bf16[1,512,2048]{2,1,0:T(8,128)(2,1)S(1)} %copy-done, f32[512,1024]{1,0:T(8,128)S(1)} %fusion), kind=kOutput, calls=%fused_computation.9 | convolution fusion | flops 1076363264 | bytes 6291456 | tf_op jit(solution)/shard_map/dot_general | solution.py:154
  156.7 10.9 %all-to-all-start.1 = ((bf16[64,8,2048]{2,1,0:T(8,128)(2,1)}), bf16[64,8,2048]{2,1,0:T(8,128)(2,1)}, u32[]{:S(2)}, u32[]{:S(2)}) async-start(bf16[64,8,2048]{2,1,0:T(8,128)(2,1)} %fusion.7), calls=%async_computation.1 | async-start | bytes 4194304 | tf_op jit(solution)/shard_map/all_to_all | solution.py:155
  167.8 0.5 fusion.23
  168.4 53.6 %all-to-all-done.1 = bf16[64,8,2048]{2,1,0:T(8,128)(2,1)} async-done(((bf16[64,8,2048]{2,1,0:T(8,128)(2,1)}), bf16[64,8,2048]{2,1,0:T(8,128)(2,1)}, u32[]{:S(2)}, u32[]{:S(2)}) %all-to-all-start.1) | async-done | bytes 2097184 | tf_op jit(solution)/shard_map/all_to_all | solution.py:155
  221.9 2.7 %fusion.11 = bf16[32,2048]{1,0:T(8,128)(2,1)S(1)} fusion(f32[32,2048]{1,0:T(8,128)S(1)} %reshape.337, f32[32,512]{1,0:T(8,128)S(1)} %fusion.23, bf16[64,8,2048]{2,1,0:T(8,128)(2,1)} %all-to-all-done.1), kind=kOutput, calls=%fused_computation.12 | convolution fusion | flops 402784256 | bytes 2555904 | tf_op jit(solution)/shard_map/dot_general | solution.py:162
  224.7 0.7 convert_element_type.85
  (59 shorter events, 1.3 us)
Async XLA Ops:
  6.5 147.6 %copy-start = (bf16[1,512,2048]{2,1,0:T(8,128)(2,1)S(1)}, bf16[1,512,2048]{2,1,0:T(8,128)(2,1)}, u32[]{:S(2)}) copy-start(bf16[1,512,2048]{2,1,0:T(8,128)(2,1)} %param.29) | copy-start | bytes 6291460
  6.5 20.7 %copy-start.1 = (bf16[8,4,16,384]{3,2,1,0:T(8,128)(2,1)S(1)}, bf16[8,4,16,384]{3,2,1,0:T(8,128)(2,1)}, u32[]{:S(2)}) copy-start(bf16[8,4,16,384]{3,2,1,0:T(8,128)(2,1)} %param.18) | copy-start | bytes 1179652
  6.5 61.7 %all-gather.2.cloned.1.call-start = ((), (), s32[]{:S(2)}) async-start(), calls=%async_computation.2 | async-start | bytes 4456448 | tf_op jit(solution)/shard_map/all_gather | solution.py:85
  26.1 1.7 copy-start.4
  27.9 2.1 copy-start.14
  27.9 2.1 copy-start.6
  28.8 5.9 %copy-start.7 = (f32[8,4,16]{2,1,0:T(4,128)S(1)}, f32[8,4,16]{2,1,0:T(4,128)}, u32[]{:S(2)}) copy-start(f32[8,4,16]{2,1,0:T(4,128)} %param.21) | copy-start | bytes 6148
  28.8 39.4 %copy-start.13 = (s32[8]{0:T(128)S(1)}, s32[8]{0:T(128)}, u32[]{:S(2)}) copy-start(s32[8]{0:T(128)} %param.17) | copy-start | bytes 100
  30.0 5.1 %copy-start.9 = (s32[320]{0:T(512)}, s32[320]{0:T(512)S(1)}, u32[]{:S(2)}) copy-start(s32[320]{0:T(512)S(1)} %get-tuple-element.70) | copy-start | bytes 3844
  30.0 5.1 %copy-start.11 = (s32[320]{0:T(512)}, s32[320]{0:T(512)S(1)}, u32[]{:S(2)}) copy-start(s32[320]{0:T(512)S(1)} %get-tuple-element.71) | copy-start | bytes 3844
  74.2 6.5 %copy-start.2 = (bf16[8,4,2048]{2,1,0:T(4,128)(2,1)S(1)}, bf16[8,4,2048]{2,1,0:T(4,128)(2,1)}, u32[]{:S(2)}) copy-start(bf16[8,4,2048]{2,1,0:T(4,128)(2,1)} %param.22) | copy-start | bytes 393220
  74.2 6.5 %copy-start.3 = (bf16[8,4,2048]{2,1,0:T(4,128)(2,1)S(1)}, bf16[8,4,2048]{2,1,0:T(4,128)(2,1)}, u32[]{:S(2)}) copy-start(bf16[8,4,2048]{2,1,0:T(4,128)(2,1)} %param.23) | copy-start | bytes 393220
  74.2 7.2 %copy-start.8 = (f32[2048]{0:T(1024)S(1)}, f32[2048]{0:T(1024)}, u32[]{:S(2)}) copy-start(f32[2048]{0:T(1024)} %param.25) | copy-start | bytes 24580
  82.3 69.4 %copy-start.15 = (bf16[1,2048,1024]{2,1,0:T(8,128)(2,1)S(1)}, bf16[1,2048,1024]{2,1,0:T(8,128)(2,1)}, u32[]{:S(2)}) copy-start(bf16[1,2048,1024]{2,1,0:T(8,128)(2,1)} %param.28) | copy-start | bytes 12582916
  156.7 10.9 %copy-start.5 = (f32[8,4,10]{2,1,0:T(4,128)S(1)}, f32[8,4,10]{2,1,0:T(4,128)}, u32[]{:S(2)}) copy-start(f32[8,4,10]{2,1,0:T(4,128)} %param.27) | copy-start | bytes 3844
  156.7 11.0 %copy-start.10 = (s32[320]{0:T(512)S(1)}, s32[320]{0:T(512)}, u32[]{:S(2)}) copy-start(s32[320]{0:T(512)} %copy-done.9) | copy-start | bytes 3844
  156.7 11.1 %copy-start.12 = (s32[320]{0:T(512)S(1)}, s32[320]{0:T(512)}, u32[]{:S(2)}) copy-start(s32[320]{0:T(512)} %copy-done.11) | copy-start | bytes 3844
  156.7 65.2 %all-to-all-start.1 = ((bf16[64,8,2048]{2,1,0:T(8,128)(2,1)}), bf16[64,8,2048]{2,1,0:T(8,128)(2,1)}, u32[]{:S(2)}, u32[]{:S(2)}) async-start(bf16[64,8,2048]{2,1,0:T(8,128)(2,1)} %fusion.7), calls=%async_computation.1 | async-start | bytes 4194304 | tf_op jit(solution)/shard_map/all_to_all | solution.py:155
Sparse Core Ops, SparseCore 0:
  10.1 58.1 all-gather.1
where the time goes:
time: 233 us; the launch traced here: 232 us
  blocking collectives  87.5 us (38%)
  waiting for transfers between devices  87.3 us (37%)
  matrix products  16.1 us (7%)
  between operations  13.8 us (6%)
  other arithmetic  13.5 us (6%)
  starting transfers between devices  10.9 us (5%)
  local copies, waits for them, and re-layouts  3.04 us (1%)
    all_to_all x1, blocking collectives, per_device(): lax.all_to_all(buffer_out, 'exp', split_axis=0, concat_axis=0, tiled=True)  69.4 us
    all_to_all x1, waiting for transfers between devices, per_device(): lax.all_to_all(expert_out.reshape(arrived.shape), 'exp', split_axis=0, co...  53.6 us
    all_gather x1, waiting for transfers between devices, per_device(): lax.all_gather(prompt_state, 'rep', axis=1, tiled=True)  33.1 us
    all_gather x1, blocking collectives, per_device(): lax.all_gather(prompt_conv, 'rep', axis=1, tiled=True)  18 us
    all_to_all x1, starting transfers between devices, per_device(): lax.all_to_all(expert_out.reshape(arrived.shape), 'exp', split_axis=0, co...  10.9 us
    add x4, other arithmetic, per_device(): reading = reading + ratio_now * intersection * writes_list[earlier_pos]  5.76 us
    dot_general x1, matrix products, per_device(): jnp.einsum('sp,phde->shde', picker, states_all, preferred_element_type=jn...  4.74 us
  transfers between devices with their start and end apart: 2, of which 2 were waited for; matrix products, arithmetic and copies ran while one was open for 4% of the time, Pallas kernels for 0%

commit v1 on v0

v1 whole, which is shorter than its diff:
```python
import jax
import jax.numpy as jnp
from jax import lax
from jax.experimental import pallas as pl
from jax.experimental.pallas import tpu as pltpu
from jax.sharding import PartitionSpec as P

MESH = pl.DeviceIdType.MESH
F32 = jnp.float32
BF16 = jnp.bfloat16

DK = 128
CH = 384
CONV = 4
FE = 512
STEPS = 4
HEADS = 16
D = 2048
HALF = 1024
RING = 8
S_DEV = 8
PG = 8
ROWS = 32
CAP = 8
TOPK = 10
EPSILON = 1e-06
VMEM_BYTES = 56 << 20

OFFS = (0, 1, 7, 2, 6, 3, 5, 4)
BACK = tuple(OFFS.index((RING - o) % RING) for o in OFFS)
FAR_FIRST = tuple(range(RING - 1, 0, -1))


def place():
    rep = lax.axis_index("rep")
    exp = lax.axis_index("exp")
    return rep // 2, lax.rem(rep, 2), exp // RING, lax.rem(exp, RING)


def swish(inputs):
    return inputs * jax.nn.sigmoid(inputs)


def iota(shape, dim):
    return lax.broadcasted_iota(jnp.int32, shape, dim)


def mixer_kernel(
    px,
    aux,
    state,
    conv,
    taps,
    head_gain,
    gate_in,
    layer_in,
    post_gain,
    residual,
    normed_in,
    got_px,
    got_aux,
    states,
    reads,
    got_reads,
    send_px,
    recv_px,
    send_aux,
    recv_aux,
    send_reads,
    recv_reads,
):
    x, c, _, _ = place()
    me = x * 2 + c
    exp = lax.axis_index("exp")

    def peer(q, core):
        odd = lax.rem(q, 2)
        offset = odd * ((q + 1) // 2) + (1 - odd) * lax.rem(RING - q // 2, RING)
        return lax.rem(x + offset, RING) * 2 + lax.rem(c + core, 2)

    pairs = [(q, core) for q in range(RING - 1, -1, -1) for core in range(2) if (q, core) != (0, 0)]
    barrier = pltpu.get_barrier_semaphore()
    for q, core in pairs:
        pl.semaphore_signal(barrier, inc=1, device_id=(peer(q, core), exp), device_id_type=MESH)
    got_px[pl.ds(me, 1)] = px[pl.ds(me, 1)]
    got_aux[pl.ds(me, 1)] = aux[pl.ds(me, 1)]
    for p in range(PG):
        states[:, p * DK : (p + 1) * DK] = state[p]
    pl.semaphore_wait(barrier, len(pairs))

    def copy_px(there, slot):
        return pltpu.make_async_remote_copy(
            src_ref=px.at[there],
            dst_ref=got_px.at[slot],
            send_sem=send_px.at[there],
            recv_sem=recv_px.at[slot],
            device_id=(there, exp),
            device_id_type=MESH,
        )

    def copy_aux(there, slot):
        return pltpu.make_async_remote_copy(
            src_ref=aux.at[there],
            dst_ref=got_aux.at[slot],
            send_sem=send_aux.at[there],
            recv_sem=recv_aux.at[slot],
            device_id=(there, exp),
            device_id_type=MESH,
        )

    def copy_reads(there, slot):
        return pltpu.make_async_remote_copy(
            src_ref=reads.at[there],
            dst_ref=got_reads.at[slot],
            send_sem=send_reads.at[there],
            recv_sem=recv_reads.at[slot],
            device_id=(there, exp),
            device_id_type=MESH,
        )

    for q, core in pairs:
        there = peer(q, core)
        copy_aux(there, me).start()
        copy_px(there, me).start()

    weights = taps[me].astype(F32)
    gain = head_gain[...]

    def features(src):
        tile = got_aux[src]
        rows = got_px[src].astype(F32)
        slot = jnp.broadcast_to(tile[:, 8:9], (S_DEV, CH))
        inputs = []
        for i in range(CONV - 1):
            window = jnp.zeros((S_DEV, CH), F32)
            for p in range(PG):
                row = jnp.broadcast_to(conv[p * 3 + i : p * 3 + i + 1, :], (S_DEV, CH))
                window = jnp.where(slot == p, row, window)
            inputs.append(window)
        for t in range(STEPS):
            inputs.append(rows[t * S_DEV : (t + 1) * S_DEV])
        queries, keys, values = [], [], []
        for t in range(STEPS):
            summed = inputs[t] * weights[0:1]
            for j in range(1, CONV):
                summed = summed + inputs[t + j] * weights[j : j + 1]
            active = swish(summed)
            q = active[:, :DK]
            k = active[:, DK : 2 * DK]
            q = q * lax.rsqrt(jnp.sum(q * q, axis=-1, keepdims=True) + EPSILON) * DK ** (-0.5)
            k = k * lax.rsqrt(jnp.sum(k * k, axis=-1, keepdims=True) + EPSILON)
            queries.append(q.astype(BF16).astype(F32))
            keys.append(k.astype(BF16).astype(F32))
            values.append(active[:, 2 * DK :].astype(BF16).astype(F32))
        return tile, queries, keys, values

    def recur(tile, queries, keys, values, projected):
        slot = jnp.broadcast_to(tile[:, 8:9], (S_DEV, DK))

        def picked(row):
            block = projected[row * S_DEV : (row + 1) * S_DEV]
            chosen = block[:, :DK]
            for p in range(1, PG):
                chosen = jnp.where(slot == p, block[:, p * DK : (p + 1) * DK], chosen)
            return chosen

        total = [tile[:, 0:1]]
        for t in range(1, STEPS):
            total.append(total[-1] + tile[:, t : t + 1])
        writes, outs = [], []
        for t in range(STEPS):
            decay = jnp.exp(total[t])
            recalled = decay * picked(STEPS + t)
            reading = decay * picked(t)
            for j in range(t):
                ratio = jnp.exp(total[t] - total[j])
                recalled = recalled + (ratio * jnp.sum(keys[j] * keys[t], axis=-1, keepdims=True)) * writes[j]
                reading = reading + (ratio * jnp.sum(keys[j] * queries[t], axis=-1, keepdims=True)) * writes[j]
            written = tile[:, STEPS + t : STEPS + t + 1] * (values[t] - recalled)
            writes.append(written)
            reading = reading + jnp.sum(keys[t] * queries[t], axis=-1, keepdims=True) * written
            mean = jnp.mean(reading * reading, axis=-1, keepdims=True)
            outs.append(reading * lax.rsqrt(mean + EPSILON) * gain)
        return jnp.concatenate(outs, axis=0).astype(BF16)

    def step(q, carry):
        first = peer(q, 0)
        second = peer(q, 1)

        @pl.when(q > 0)
        def _():
            copy_aux(first, first).wait_recv()
            copy_px(first, first).wait_recv()

        copy_aux(second, second).wait_recv()
        copy_px(second, second).wait_recv()
        parts = [features(first), features(second)]
        stacked = jnp.concatenate([v for part in parts for v in part[1] + part[2]], axis=0).astype(BF16)
        projected = jnp.dot(stacked, states[...], preferred_element_type=F32)
        for i, src in enumerate((first, second)):
            reads[pl.ds(src, 1)] = recur(*parts[i], projected[i * 64 : (i + 1) * 64])[None]

        @pl.when(q > 0)
        def _():
            copy_reads(first, me).start()

        copy_reads(second, me).start()
        return carry

    lax.fori_loop(0, RING, step, 0)
    got_reads[pl.ds(me, 1)] = reads[pl.ds(me, 1)]
    for q, core in pairs[::-1]:
        there = peer(q, core)
        copy_reads(there, there).wait_recv()

    row, col = iota((ROWS, ROWS), 0), iota((ROWS, ROWS), 1)
    order = ((row // STEPS == lax.rem(col, S_DEV)) & (lax.rem(row, STEPS) == col // S_DEV)).astype(BF16)
    squares = jnp.zeros((ROWS, 1), F32)
    for h in range(HEADS):
        lanes = slice(h * DK, (h + 1) * DK)
        normed = jnp.dot(order, got_reads[h], preferred_element_type=F32)
        value = layer_in[:, lanes].astype(F32) + normed * swish(gate_in[:, lanes].astype(F32))
        residual[:, lanes] = value
        squares = squares + jnp.sum(value * value, axis=-1, keepdims=True)
    scale = lax.rsqrt(squares / D + EPSILON)
    for half in range(2):
        lanes = slice(half * HALF, (half + 1) * HALF)
        normed_in[half] = (residual[:, lanes] * scale * post_gain[:, lanes]).astype(BF16)

    for q, core in pairs:
        there = peer(q, core)
        copy_aux(there, me).wait_send()
        copy_px(there, me).wait_send()
        copy_reads(there, me).wait_send()


def experts_kernel(
    rows_in,
    residual,
    ids,
    route,
    gate_up_hbm,
    down_hbm,
    out,
    gate_up,
    down,
    info_out,
    info_in,
    near,
    pick,
    mix_hi,
    mix_lo,
    slots_out,
    slots_in,
    hidden_sum,
    hidden,
    back_out,
    back_in,
    part_out,
    part_in,
    load_sem,
    send_sem,
    recv_sem,
):
    _, _, y, z = place()
    rep = lax.axis_index("rep")

    def along_y(o):
        return (rep, lax.rem(y + o, RING) * RING + z)

    def along_z(o):
        return (rep, y * RING + lax.rem(z + o, RING))

    first_axis, second_axis = (along_y, along_z), (along_z, along_y)

    load_gate_up = pltpu.make_async_copy(gate_up_hbm, gate_up, load_sem.at[0])
    load_down = pltpu.make_async_copy(down_hbm, down, load_sem.at[1])
    load_gate_up.start()
    load_down.start()
    barrier = pltpu.get_barrier_semaphore()
    for q in FAR_FIRST:
        for axis in (along_y, along_z):
            pl.semaphore_signal(barrier, inc=1, device_id=axis(OFFS[q]), device_id_type=MESH)

    def copy(phase, half, axis, q, src, dst):
        return pltpu.make_async_remote_copy(
            src_ref=src(q),
            dst_ref=dst(BACK[q]),
            send_sem=send_sem.at[phase * 2 + half, q],
            recv_sem=recv_sem.at[phase * 2 + half, BACK[q]],
            device_id=axis(OFFS[q]),
            device_id_type=MESH,
        )

    def blocks(ref, half, size):
        return lambda q: ref.at[half, pl.ds(q * size, size)]

    def info_copy(half, q):
        return copy(0, half, first_axis[half], q, lambda i: info_out.at[half, i], lambda i: info_in.at[half, i])

    def row_copy(half, q):
        return copy(1, half, first_axis[half], q, lambda i: rows_in.at[half], blocks(near, half, ROWS))

    def slot_copy(half, q):
        return copy(2, half, second_axis[half], q, blocks(slots_out, half, 64), blocks(slots_in, half, 64))

    def back_copy(half, q):
        return copy(3, half, second_axis[half], q, blocks(back_out, half, 64), blocks(back_in, half, 64))

    def part_copy(half, q):
        return copy(4, half, first_axis[half], q, blocks(part_out, half, ROWS), blocks(part_in, half, ROWS))

    def arrived(copy_of, half, q):
        copy_of(half, BACK[q]).wait_recv()

    def offset_of(position):
        value = jnp.zeros_like(position)
        for i, o in enumerate(OFFS):
            value = jnp.where(position == i, o, value)
        return value

    def back_of(position):
        value = jnp.zeros_like(position)
        for i, o in enumerate(BACK):
            value = jnp.where(position == i, o, value)
        return value

    shape = (64, 128)
    q_of, m_of = iota(shape, 0) // RING, lax.rem(iota(shape, 0), RING)
    lane_block = iota(shape, 1) // ROWS
    mine = lane_block == lax.rem(back_of(q_of), 4)
    near_o, far_o = offset_of(q_of), offset_of(m_of)
    for half in range(2):
        y_o, z_o = (near_o, far_o) if half == 0 else (far_o, near_o)
        expert = lax.rem(y + y_o, RING) * RING + lax.rem(z + z_o, RING)
        weight = jnp.zeros(shape, F32)
        for k in range(TOPK):
            weight = weight + jnp.where(ids[k : k + 1, :] == expert, route[k : k + 1, :], 0.0)
        weight = jnp.where(mine, weight, 0.0)
        info_out[half] = weight.reshape(RING, RING, 128)
        info_in[half, 0] = weight[:RING]
        near[half, 0:ROWS] = rows_in[half]

    pl.semaphore_wait(barrier, 2 * (RING - 1))
    for q in FAR_FIRST:
        for half in range(2):
            info_copy(half, q).start()
            row_copy(half, q).start()

    cols = RING * ROWS
    before = (
        (iota((cols, cols), 0) // ROWS == iota((cols, cols), 1) // ROWS)
        & (iota((cols, cols), 0) < iota((cols, cols), 1))
    ).astype(BF16)
    pick_rows = iota((64, cols), 0)
    diagonal = pick_rows // CAP == iota((64, cols), 1) // ROWS
    slot_of = lax.rem(pick_rows, CAP).astype(F32)
    for half in range(2):
        for q in range(1, RING):
            arrived(info_copy, half, q)
        low = info_in[half, 0] + info_in[half, 1] + info_in[half, 2] + info_in[half, 3]
        high = info_in[half, 4] + info_in[half, 5] + info_in[half, 6] + info_in[half, 7]
        weight = jnp.concatenate([low, high], axis=1)
        named = (weight > 0.0).astype(BF16)
        position = jnp.dot(named, before, preferred_element_type=F32)
        for pair in range(4):
            mixes = []
            for m in (2 * pair, 2 * pair + 1):
                w = jnp.broadcast_to(weight[m : m + 1], (64, cols))
                at = jnp.broadcast_to(position[m : m + 1], (64, cols))
                hit = diagonal & (at == slot_of) & (w > 0.0)
                pick[half, m * 64 : (m + 1) * 64] = hit.astype(F32).astype(BF16)
                mixes.append(jnp.where(hit, w, 0.0))
            mix = jnp.transpose(jnp.concatenate(mixes, axis=0))
            top = mix.astype(BF16)
            lanes = slice(pair * 128, (pair + 1) * 128)
            mix_hi[half, :, lanes] = top
            mix_lo[half, :, lanes] = (mix - top.astype(F32)).astype(BF16)

    for half in range(2):
        for q in range(1, RING):
            arrived(row_copy, half, q)
    for pair in range(3, -1, -1):
        for half in range(2):
            span = slice(pair * 128, (pair + 1) * 128)
            chosen = jnp.dot(pick[half, span], near[half], preferred_element_type=F32).astype(BF16)
            slots_out[half, span] = chosen
            if pair == 0:
                slots_in[half, 0:64] = chosen[0:64]
            for m in (2 * pair + 1, 2 * pair):
                if m:
                    slot_copy(half, m).start()

    load_gate_up.wait()
    for half in range(2):
        for m in range(1, RING):
            arrived(slot_copy, half, m)

        def up(n, carry, half=half):
            lanes = pl.ds(pl.multiple_of(n * 256, 256), 256)
            hidden_sum[half, :, lanes] = jnp.dot(
                slots_in[half], gate_up[half * HALF : (half + 1) * HALF, lanes], preferred_element_type=F32
            )
            return carry

        lax.fori_loop(0, 2 * FE // 256, up, 0)

    def activate(m, carry):
        for q in range(RING):
            here = pl.ds(pl.multiple_of(m * 64 + q * CAP, CAP), CAP)
            turned = pl.ds(pl.multiple_of(q * 64 + m * CAP, CAP), CAP)
            both = hidden_sum[0, here] + hidden_sum[1, turned]
            value = swish(both[:, :FE]) * both[:, FE:]
            hidden[0, here] = value
            hidden[1, turned] = value
        return carry

    lax.fori_loop(0, RING, activate, 0)
    load_down.wait()
    for pair in range(3, -1, -1):
        for half in range(2):
            span = slice(pair * 128, (pair + 1) * 128)
            value = jnp.dot(
                hidden[half, span].astype(BF16),
                down[:, half * HALF : (half + 1) * HALF],
                preferred_element_type=F32,
            ).astype(BF16)
            back_out[half, span] = value
            if pair == 0:
                back_in[half, 0:64] = value[0:64]
            for m in (2 * pair + 1, 2 * pair):
                if m:
                    back_copy(half, m).start()

    for half in range(2):
        for m in range(1, RING):
            arrived(back_copy, half, m)
        parts = jnp.dot(mix_hi[half], back_in[half], preferred_element_type=F32)
        parts = parts + jnp.dot(mix_lo[half], back_in[half], preferred_element_type=F32)
        part_out[half] = parts.astype(BF16)
        for q in FAR_FIRST:
            part_copy(half, q).start()
    for half in range(2):
        lanes = slice(half * HALF, (half + 1) * HALF)
        total = residual[:, lanes] + part_out[half, 0:ROWS].astype(F32)
        for q in range(1, RING):
            arrived(part_copy, half, q)
            total = total + part_in[half, q * ROWS : (q + 1) * ROWS].astype(F32)
        out[:, lanes] = total.astype(BF16)

    for half in range(2):
        for q in range(1, RING):
            for copy_of in (info_copy, row_copy, slot_copy, back_copy, part_copy):
                copy_of(half, q).wait_send()


def per_device(
    prompt_state,
    prompt_conv,
    slot_prompt,
    projected,
    conv_weight,
    log_decay,
    write_rate,
    gate_in,
    layer_in,
    head_gain,
    post_gain,
    expert_ids,
    route_weight,
    w_gate_up,
    w_down,
):
    vmem = pl.BlockSpec(memory_space=pltpu.VMEM)
    hbm = pl.BlockSpec(memory_space=pl.ANY)
    dma = pltpu.SemaphoreType.DMA

    px = jnp.transpose(projected, (2, 1, 0, 3)).reshape(HEADS, ROWS, CH)
    slots = jnp.broadcast_to(slot_prompt.astype(F32)[None, :, None], (HEADS, S_DEV, 1))
    aux = jnp.concatenate(
        [jnp.transpose(log_decay, (2, 0, 1)), jnp.transpose(write_rate, (2, 0, 1)), slots], axis=2
    )
    aux = jnp.pad(aux, ((0, 0), (0, 0), (0, 128 - aux.shape[2])))
    residual, normed_in = pl.pallas_call(
        mixer_kernel,
        out_shape=(
            jax.ShapeDtypeStruct((ROWS, D), F32),
            jax.ShapeDtypeStruct((2, ROWS, HALF), BF16),
        ),
        in_specs=[vmem] * 9,
        out_specs=(vmem, vmem),
        scratch_shapes=[
            pltpu.VMEM((HEADS, ROWS, CH), BF16),
            pltpu.VMEM((HEADS, S_DEV, 128), F32),
            pltpu.VMEM((DK, PG * DK), BF16),
            pltpu.VMEM((HEADS, ROWS, DK), BF16),
            pltpu.VMEM((HEADS, ROWS, DK), BF16),
        ]
        + [dma((HEADS,))] * 6,
        compiler_params=pltpu.CompilerParams(
            collective_id=0, has_side_effects=True, vmem_limit_bytes=VMEM_BYTES
        ),
        name="mixer",
    )(
        px,
        aux,
        prompt_state.reshape(PG, DK, DK),
        prompt_conv.reshape(PG * 3, CH).astype(F32),
        conv_weight,
        head_gain.reshape(1, DK),
        gate_in.reshape(ROWS, D),
        layer_in.reshape(ROWS, D),
        post_gain.reshape(1, D),
    )

    ids = jnp.tile(jnp.transpose(expert_ids.reshape(ROWS, TOPK)), (1, 4))
    route = jnp.tile(jnp.transpose(route_weight.reshape(ROWS, TOPK)), (1, 4))
    out = pl.pallas_call(
        experts_kernel,
        out_shape=jax.ShapeDtypeStruct((ROWS, D), BF16),
        in_specs=[vmem] * 4 + [hbm] * 2,
        out_specs=vmem,
        scratch_shapes=[
            pltpu.VMEM((D, 2 * FE), BF16),
            pltpu.VMEM((FE, D), BF16),
            pltpu.VMEM((2, RING, RING, 128), F32),
            pltpu.VMEM((2, RING, RING, 128), F32),
            pltpu.VMEM((2, RING * ROWS, HALF), BF16),
            pltpu.VMEM((2, 512, RING * ROWS), BF16),
            pltpu.VMEM((2, RING * ROWS, 512), BF16),
            pltpu.VMEM((2, RING * ROWS, 512), BF16),
            pltpu.VMEM((2, 512, HALF), BF16),
            pltpu.VMEM((2, 512, HALF), BF16),
            pltpu.VMEM((2, 512, 2 * FE), F32),
            pltpu.VMEM((2, 512, FE), F32),
            pltpu.VMEM((2, 512, HALF), BF16),
            pltpu.VMEM((2, 512, HALF), BF16),
            pltpu.VMEM((2, RING * ROWS, HALF), BF16),
            pltpu.VMEM((2, RING * ROWS, HALF), BF16),
            dma((2,)),
            dma((10, RING)),
            dma((10, RING)),
        ],
        compiler_params=pltpu.CompilerParams(
            collective_id=1, has_side_effects=True, vmem_limit_bytes=VMEM_BYTES
        ),
        name="experts",
    )(normed_in, residual, ids, route, w_gate_up.reshape(D, 2 * FE), w_down.reshape(FE, D))
    return out.reshape(layer_in.shape)


def solution(mesh):
    rows = ("rep", "exp")
    in_specs = (
        P("exp", "rep", None, None),
        P("exp", "rep", None, None),
        P(rows),
        P(rows, None, None, None),
        P(),
        P(rows, None, None),
        P(rows, None, None),
        P(rows, None, None),
        P(rows, None, None),
        P(),
        P(),
        P(rows, None, None),
        P(rows, None, None),
        P("exp", None, None),
        P("exp", None, None),
    )
    return jax.shard_map(
        per_device, mesh=mesh, in_specs=in_specs, out_specs=P(rows, None, None), check_vma=False
    )
```

time: 233 us -> 152 us (0.65)
  the two profiles are of different devices: /device:TPU:48 before, /device:TPU:1 now
where the time goes in v1:
time: 152 us; the launch traced here: 151 us
  Pallas kernels  137 us (90%)
  local copies, waits for them, and re-layouts  12.9 us (8%)
    pallas_call x1, Pallas kernels, per_device(): pl.pallas_call(experts_kernel, out_shape=jax.ShapeDtypeStruct((ROWS, D),...  94.3 us
    pallas_call x1, Pallas kernels, per_device(): pl.pallas_call(mixer_kernel, out_shape=(jax.ShapeDtypeStruct((ROWS, D), F...  42.6 us

profile of v1, /device:TPU:1, one launch (start us, length us, event | category | flops | bytes accessed | tf_op | source)
XLA Modules:
  0.0 151.2 jit_solution(13450321402270348768)
XLA Ops:
  0.0 2.0 %copy.29 = bf16[16,4,8,384]{3,2,1,0:T(8,128)(2,1)} copy(bf16[16,4,8,384]{3,0,1,2:T(8,128)(2,1)} %bitcast.22) | data formatting | bytes 786432 | tf_op jit(solution)/shard_map/transpose | solution.py:478
  2.0 0.7 convert_element_type.10
  2.6 0.1 broadcast_in_dim.2
  2.7 0.8 copy.23
  3.5 0.8 copy.24
  4.4 0.7 select_maximum_fusion.aux
  5.1 1.6 %reshape.50.gate_in = bf16[32,2048]{1,0:T(8,128)(2,1)} reshape(bf16[8,4,2048]{2,1,0:T(4,128)(2,1)} %param.22) | data formatting | bytes 262144 | tf_op jit(solution)/shard_map/reshape | solution.py:511
  6.7 1.6 %reshape.51.layer_in = bf16[32,2048]{1,0:T(8,128)(2,1)} reshape(bf16[8,4,2048]{2,1,0:T(4,128)(2,1)} %param.23) | data formatting | bytes 262144 | tf_op jit(solution)/shard_map/reshape | solution.py:512
  8.3 0.7 copy.25
  9.0 0.6 reshape.58.conv
  9.7 42.6 %mixer.1 = (f32[32,2048]{1,0:T(8,128)}, bf16[2,32,1024]{2,1,0:T(8,128)(2,1)}) custom-call(bf16[16,32,384]{2,1,0:T(8,128)(2,1)} %bitcast.21, f32[16,8,128]{2,1,0:T(8,128)} %select_maximum_fusion.aux, bf16[8,128,128]{2,1,0:T(8,128)(2,1)} %bitcast.25, f32[24,384]{1,0:T(8,128)} %reshape.58.conv, bf16[16,4,384]{2,1,0:T(4,128)(2,1)} %taps.1, f32[1,128]{1,0:T(1,128)} %bitcast.29, ...), custom_call_target="tpu_custom_call" | custom-call | tf_op jit(solution)/shard_map/mixer/pallas_call | solution.py:484
  52.2 0.8 copy.27
  53.1 0.7 tile.21.route
  53.7 0.8 copy.26
  54.5 0.7 tile.9.ids
  55.2 94.3 %experts.1 = bf16[32,2048]{1,0:T(8,128)(2,1)} custom-call(bf16[2,32,1024]{2,1,0:T(8,128)(2,1)} %get-tuple-element.7.rows_in, f32[32,2048]{1,0:T(8,128)} %get-tuple-element.8.residual, s32[10,128]{1,0:T(8,128)} %tile.9.ids, f32[10,128]{1,0:T(8,128)} %tile.21.route, bf16[2048,1024]{1,0:T(8,128)(2,1)} %bitcast.19, bf16[512,2048]{1,0:T(8,128)(2,1)} %bitcast.20), custom_call_target="tpu_custom_call" | custom-call | tf_op jit(solution)/shard_map/experts/pallas_call | solution.py:518
  149.6 1.6 %reshape.57 = bf16[8,4,2048]{2,1,0:T(4,128)(2,1)} reshape(bf16[32,2048]{1,0:T(8,128)(2,1)} %experts.1) | data formatting | bytes 262144 | tf_op jit(solution)/shard_map/reshape | solution.py:549
  (2 shorter events, 0.0 us)

commit v2 on v0

v2 whole, which is shorter than its diff:
```python
import jax
import jax.numpy as jnp
from jax import lax
from jax.experimental import pallas as pl
from jax.experimental.pallas import tpu as pltpu
from jax.sharding import PartitionSpec as P

MESH = pl.DeviceIdType.MESH
F32 = jnp.float32
BF16 = jnp.bfloat16

DK = 128
CH = 384
CONV = 4
FE = 512
STEPS = 4
HEADS = 16
D = 2048
HALF = 1024
PART = 512
RING = 8
S_DEV = 8
PG = 8
ROWS = 32
CAP = 8
TOPK = 10
EPSILON = 1e-06
VMEM_BYTES = 56 << 20

OFFS = (0, 1, 7, 2, 6, 3, 5, 4)
BACK = tuple(OFFS.index((RING - o) % RING) for o in OFFS)
FAR_FIRST = tuple(range(RING - 1, 0, -1))


def place():
    rep = lax.axis_index("rep")
    exp = lax.axis_index("exp")
    return rep // 2, lax.rem(rep, 2), exp // RING, lax.rem(exp, RING)


def swish(inputs):
    return inputs * jax.nn.sigmoid(inputs)


def iota(shape, dim):
    return lax.broadcasted_iota(jnp.int32, shape, dim)


def layer_kernel(
    projected_in,
    slot_prompt,
    log_decay,
    write_rate,
    state,
    conv,
    taps,
    head_gain,
    gate_in,
    layer_in,
    post_gain,
    ids,
    route,
    gate_up_hbm,
    down_hbm,
    out,
    gate_up,
    down,
    px,
    aux,
    got_px,
    got_aux,
    states,
    kept,
    reads,
    got_reads,
    gate,
    residual,
    rows_out,
    info_out,
    info_in,
    near,
    pick,
    mix_in,
    slots_out,
    slots_in,
    hidden_sum,
    hidden,
    back_out,
    back_in,
    part_out,
    part_in,
    load_sem,
    send_x,
    recv_x,
    send_sem,
    recv_sem,
):
    x, c, y, z = place()
    me = x * 2 + c
    exp = lax.axis_index("exp")

    load_gate_up = pltpu.make_async_copy(gate_up_hbm, gate_up, load_sem.at[0])
    load_down = pltpu.make_async_copy(down_hbm, down, load_sem.at[1])

    def peer(q, core):
        odd = lax.rem(q, 2)
        offset = odd * ((q + 1) // 2) + (1 - odd) * lax.rem(RING - q // 2, RING)
        return lax.rem(x + offset, RING) * 2 + lax.rem(c + core, 2)

    def along_y(o):
        return (me, lax.rem(y + o, RING) * RING + z)

    def along_z(o):
        return (me, y * RING + lax.rem(z + o, RING))

    first_axis, second_axis = (along_y, along_z), (along_z, along_y)

    pairs = [(q, core) for q in range(RING - 1, -1, -1) for core in range(2) if (q, core) != (0, 0)]
    barrier = pltpu.get_barrier_semaphore()
    for q, core in pairs:
        pl.semaphore_signal(barrier, inc=1, device_id=(peer(q, core), exp), device_id_type=MESH)
    for q in FAR_FIRST:
        for axis in (along_y, along_z):
            pl.semaphore_signal(barrier, inc=1, device_id=axis(OFFS[q]), device_id_type=MESH)
    load_gate_up.start()
    load_down.start()

    def x_copy(kind, src, dst, there, slot):
        return pltpu.make_async_remote_copy(
            src_ref=src,
            dst_ref=dst,
            send_sem=send_x.at[kind, there],
            recv_sem=recv_x.at[kind, slot],
            device_id=(there, exp),
            device_id_type=MESH,
        )

    def copy_aux(there, slot):
        return x_copy(0, aux.at[there], got_aux.at[slot], there, slot)

    def copy_px(u, there, slot):
        return x_copy(1 + u, px.at[u, there], got_px.at[u, slot], there, slot)

    def copy_reads(u, there, slot):
        return x_copy(3 + u, reads.at[u, there], got_reads.at[u, slot], there, slot)

    tile_lane = iota((S_DEV, 128), 1)
    diagonal8 = iota((S_DEV, S_DEV), 0) == iota((S_DEV, S_DEV), 1)
    slot_row = jnp.broadcast_to(slot_prompt[...].astype(F32).reshape(1, S_DEV), (S_DEV, S_DEV))
    slot_column = jnp.sum(jnp.where(diagonal8, slot_row, 0.0), axis=-1, keepdims=True)
    scalars = jnp.concatenate(
        [log_decay[:, t, :] for t in range(STEPS)] + [write_rate[:, t, :] for t in range(STEPS)], axis=1
    )
    for h in range(HEADS):
        turned = scalars if h == 0 else pltpu.roll(scalars, 128 - h, 1)
        aux[h] = jnp.where(tile_lane == 1, slot_column, turned)

    for u in range(2):
        turned = [jnp.swapaxes(projected_in[:, 2 * u + i].astype(F32), 0, 1) for i in range(2)]
        px[u] = jnp.concatenate(turned, axis=1).astype(BF16)

    pl.semaphore_wait(barrier, len(pairs) + 2 * (RING - 1))
    for q, core in pairs:
        there = peer(q, core)
        copy_aux(there, me).start()
        copy_px(0, there, me).start()

    got_aux[pl.ds(me, 1)] = aux[pl.ds(me, 1)]
    for u in range(2):
        got_px[u, pl.ds(me, 1)] = px[u, pl.ds(me, 1)]
    for p in range(PG):
        states[:, p * DK : (p + 1) * DK] = state[p]
    for t in range(STEPS):
        span = slice(t * S_DEV, (t + 1) * S_DEV)
        gate[span] = swish(gate_in[:, t, :].astype(F32))
        residual[span] = layer_in[:, t, :].astype(F32)

    def copy(phase, half, axis, q, src, dst):
        return pltpu.make_async_remote_copy(
            src_ref=src(q),
            dst_ref=dst(BACK[q]),
            send_sem=send_sem.at[phase * 2 + half, q],
            recv_sem=recv_sem.at[phase * 2 + half, BACK[q]],
            device_id=axis(OFFS[q]),
            device_id_type=MESH,
        )

    def info_copy(half, q):
        return copy(0, half, first_axis[half], q, lambda i: info_out.at[half, i], lambda i: info_in.at[half, i])

    def chunk_copy(phase, axes, out_ref, in_ref, size):
        def of_chunk(ch):
            def of(half, q):
                src = lambda i: out_ref.at[half, ch, pl.ds(i * size, size)]
                dst = lambda i: in_ref.at[half, ch, pl.ds(i * size, size)]
                return copy(phase + ch, half, axes[half], q, src, dst)

            return of

        return of_chunk

    slot_copy = chunk_copy(3, second_axis, slots_out, slots_in, 64)
    back_copy = chunk_copy(5, second_axis, back_out, back_in, 64)
    part_copy = chunk_copy(7, first_axis, part_out, part_in, ROWS)

    def row_copy(u):
        def of(half, q):
            src = lambda i: rows_out.at[half, pl.ds(u * 16, 16)]
            dst = lambda i: near.at[half, pl.ds(i * ROWS + u * 16, 16)]
            return copy(1 + u, half, first_axis[half], q, src, dst)

        return of

    def arrived(copy_of, half, q):
        copy_of(half, BACK[q]).wait_recv()

    def looked_up(table, position):
        value = jnp.zeros_like(position)
        for i, o in enumerate(table):
            value = jnp.where(position == i, o, value)
        return value

    lane = iota((1, 128), 1)
    near_o = looked_up(OFFS, lax.rem(lane // RING, RING))
    far_o = looked_up(OFFS, lax.rem(lane, RING))
    y_o = jnp.where(lane < 64, near_o, far_o)
    z_o = jnp.where(lane < 64, far_o, near_o)
    expert = lax.rem(y + y_o, RING) * RING + lax.rem(z + z_o, RING)
    named = []
    for t in range(STEPS):
        ids_t, route_t = ids[:, t, :], route[:, t, :]
        weight = jnp.zeros((S_DEV, 128), F32)
        for k in range(TOPK):
            weight = weight + jnp.where(ids_t[:, k : k + 1] == expert, route_t[:, k : k + 1], 0.0)
        named.append(weight)
    turned = jnp.transpose(jnp.concatenate(named * 4, axis=0))
    shape = (128, 128)
    mine = iota(shape, 1) // ROWS == lax.rem(looked_up(BACK, lax.rem(iota(shape, 0) // RING, RING)), 4)
    turned = jnp.where(mine, turned, 0.0)
    for half in range(2):
        weight = turned[half * 64 : (half + 1) * 64]
        info_out[half] = weight.reshape(RING, RING, 128)
        info_in[half, 0] = weight[:RING]
        for q in FAR_FIRST:
            info_copy(half, q).start()

    weights = taps[me].astype(F32)
    gain = head_gain[...]
    history = [conv[i].astype(F32) for i in range(CONV - 1)]

    def features(u, src):
        tile = got_aux[src]
        rows = [got_px[v, src].astype(F32) for v in range(u + 1)]
        rows = [part[i * S_DEV : (i + 1) * S_DEV] for part in rows for i in range(2)]
        slot = jnp.broadcast_to(tile[:, 1:2], (S_DEV, CH))
        inputs = []
        for i in range(2 * u, CONV - 1):
            window = jnp.broadcast_to(history[i][0:1], (S_DEV, CH))
            for p in range(1, PG):
                window = jnp.where(slot == p, jnp.broadcast_to(history[i][p : p + 1], (S_DEV, CH)), window)
            inputs.append(window)
        inputs = inputs + rows
        queries, keys, values = [], [], []
        for t in range(2):
            summed = inputs[t] * weights[0:1]
            for j in range(1, CONV):
                summed = summed + inputs[t + j] * weights[j : j + 1]
            active = swish(summed)
            q = active[:, :DK]
            k = active[:, DK : 2 * DK]
            q = q * lax.rsqrt(jnp.sum(q * q, axis=-1, keepdims=True) + EPSILON) * DK ** (-0.5)
            k = k * lax.rsqrt(jnp.sum(k * k, axis=-1, keepdims=True) + EPSILON)
            queries.append(q.astype(BF16).astype(F32))
            keys.append(k.astype(BF16).astype(F32))
            values.append(active[:, 2 * DK :].astype(BF16).astype(F32))
        return tile, queries, keys, values

    def recur(u, src, tile, queries, keys, values, projected):
        slot = jnp.broadcast_to(tile[:, 1:2], (S_DEV, DK))

        def picked(row):
            block = projected[row * S_DEV : (row + 1) * S_DEV]
            chosen = block[:, :DK]
            for p in range(1, PG):
                chosen = jnp.where(slot == p, block[:, p * DK : (p + 1) * DK], chosen)
            return chosen

        def column(i):
            return tile[:, i * 16 : i * 16 + 1]

        total = [column(0)]
        for t in range(1, 2 * u + 2):
            total.append(total[-1] + column(t))
        old_keys, writes = [], []
        if u:
            before = kept[src]
            old_keys, writes = [before[0], before[1]], [before[2], before[3]]
        all_keys = old_keys + keys
        outs = []
        for i in range(2):
            t = 2 * u + i
            decay = jnp.exp(total[t])
            recalled = decay * picked(2 + i)
            reading = decay * picked(i)
            for j in range(t):
                ratio = jnp.exp(total[t] - total[j])
                recalled = recalled + (ratio * jnp.sum(all_keys[j] * keys[i], axis=-1, keepdims=True)) * writes[j]
                reading = reading + (ratio * jnp.sum(all_keys[j] * queries[i], axis=-1, keepdims=True)) * writes[j]
            written = column(STEPS + t) * (values[i] - recalled)
            writes.append(written)
            reading = reading + jnp.sum(keys[i] * queries[i], axis=-1, keepdims=True) * written
            mean = jnp.mean(reading * reading, axis=-1, keepdims=True)
            outs.append(reading * lax.rsqrt(mean + EPSILON) * gain)
        if not u:
            for i, value in enumerate(keys + writes):
                kept[src, i] = value
        return jnp.concatenate(outs, axis=0).astype(BF16)

    def heads_step(u):
        def step(q, carry):
            first = peer(q, 0)
            second = peer(q, 1)

            @pl.when(q > 0)
            def _():
                if u == 0:
                    copy_aux(first, first).wait_recv()
                copy_px(u, first, first).wait_recv()

            if u == 0:
                copy_aux(second, second).wait_recv()
            copy_px(u, second, second).wait_recv()
            parts = [features(u, first), features(u, second)]
            stacked = jnp.concatenate([v for part in parts for v in part[1] + part[2]], axis=0).astype(BF16)
            projected = jnp.dot(stacked, states[...], preferred_element_type=F32)
            for i, src in enumerate((first, second)):
                reads[u, pl.ds(src, 1)] = recur(u, src, *parts[i], projected[i * 32 : (i + 1) * 32])[None]

            @pl.when(q > 0)
            def _():
                copy_reads(u, first, me).start()
                if u == 0:
                    copy_px(1, first, me).start()

            copy_reads(u, second, me).start()
            if u == 0:
                copy_px(1, second, me).start()
            return carry

        return step

    def mix(u):
        got_reads[u, pl.ds(me, 1)] = reads[u, pl.ds(me, 1)]
        for q, core in pairs[::-1]:
            there = peer(q, core)
            copy_reads(u, there, there).wait_recv()
        span = slice(u * 16, (u + 1) * 16)
        squares = jnp.zeros((16, 128), F32)
        for h in range(HEADS):
            lanes = slice(h * DK, (h + 1) * DK)
            value = residual[span, lanes] + got_reads[u, h].astype(F32) * gate[span, lanes]
            residual[span, lanes] = value
            squares = squares + value * value
        scale = lax.rsqrt(jnp.sum(squares, axis=-1, keepdims=True) / D + EPSILON)
        for half in range(2):
            lanes = slice(half * HALF, (half + 1) * HALF)
            value = (residual[span, lanes] * scale * post_gain[:, lanes]).astype(BF16)
            rows_out[half, span] = value
            near[half, span] = value
        for q in FAR_FIRST:
            for half in range(2):
                row_copy(u)(half, q).start()

    lax.fori_loop(0, RING, heads_step(0), 0)
    lax.fori_loop(0, RING // 2, heads_step(1), 0)
    mix(0)
    lax.fori_loop(RING // 2, RING, heads_step(1), 0)

    cols = RING * ROWS
    earlier = (
        (iota((cols, cols), 0) // ROWS == iota((cols, cols), 1) // ROWS)
        & (iota((cols, cols), 0) < iota((cols, cols), 1))
    ).astype(BF16)
    pick_rows = iota((64, cols), 0)
    diagonal = pick_rows // CAP == iota((64, cols), 1) // ROWS
    slot_of = lax.rem(pick_rows, CAP).astype(F32)
    route_in = []
    for half in range(2):
        for q in range(1, RING):
            arrived(info_copy, half, q)
        low = info_in[half, 0] + info_in[half, 1] + info_in[half, 2] + info_in[half, 3]
        high = info_in[half, 4] + info_in[half, 5] + info_in[half, 6] + info_in[half, 7]
        weight = jnp.concatenate([low, high], axis=1)
        position = jnp.dot((weight > 0.0).astype(BF16), earlier, preferred_element_type=F32)
        route_in.append((weight, position))

    def hits(half, m):
        weight, position = route_in[half]
        w = jnp.broadcast_to(weight[m : m + 1], (64, cols))
        at = jnp.broadcast_to(position[m : m + 1], (64, cols))
        return diagonal & (at == slot_of) & (w > 0.0), w

    mix(1)
    for half in range(2):
        for m in range(RING):
            pick[half, m * 64 : (m + 1) * 64] = hits(half, m)[0].astype(F32).astype(BF16)

    for half in range(2):
        for q in range(1, RING):
            arrived(row_copy(0), half, q)
            arrived(row_copy(1), half, q)
    for ch in range(2):
        lanes = slice(ch * PART, (ch + 1) * PART)
        for half in range(2):
            chosen = jnp.dot(pick[half], near[half, :, lanes], preferred_element_type=F32).astype(BF16)
            slots_out[half, ch] = chosen
            slots_in[half, ch, 0:64] = chosen[0:64]
            for m in FAR_FIRST:
                slot_copy(ch)(half, m).start()

    for half in range(2):
        for pair in range(4):
            mixes = []
            for m in (2 * pair, 2 * pair + 1):
                hit, w = hits(half, m)
                mixes.append(jnp.where(hit, w, 0.0))
            turned = jnp.transpose(jnp.concatenate(mixes, axis=0))
            mix_in[half, :, pair * 128 : (pair + 1) * 128] = turned.astype(BF16)

    load_gate_up.wait()
    for ch in range(2):
        for half in range(2):
            for m in range(1, RING):
                arrived(slot_copy(ch), half, m)

            def up(n, carry, half=half, ch=ch):
                lanes = pl.ds(pl.multiple_of(n * 256, 256), 256)
                depth = slice(half * HALF + ch * PART, half * HALF + (ch + 1) * PART)
                product = jnp.dot(slots_in[half, ch], gate_up[depth, lanes], preferred_element_type=F32)
                if ch:
                    product = product + hidden_sum[half, :, lanes]
                hidden_sum[half, :, lanes] = product
                return carry

            lax.fori_loop(0, 2 * FE // 256, up, 0)

    def activate(m, carry):
        for q in range(RING):
            here = pl.ds(pl.multiple_of(m * 64 + q * CAP, CAP), CAP)
            turned = pl.ds(pl.multiple_of(q * 64 + m * CAP, CAP), CAP)
            both = hidden_sum[0, here] + hidden_sum[1, turned]
            value = swish(both[:, :FE]) * both[:, FE:]
            hidden[0, here] = value
            hidden[1, turned] = value
        return carry

    lax.fori_loop(0, RING, activate, 0)
    load_down.wait()
    for ch in range(2):
        for half in range(2):
            lanes = slice(half * HALF + ch * PART, half * HALF + (ch + 1) * PART)
            value = jnp.dot(hidden[half].astype(BF16), down[:, lanes], preferred_element_type=F32).astype(BF16)
            back_out[half, ch] = value
            back_in[half, ch, 0:64] = value[0:64]
            for m in FAR_FIRST:
                back_copy(ch)(half, m).start()

    for ch in range(2):
        for half in range(2):
            for m in range(1, RING):
                arrived(back_copy(ch), half, m)
            parts = jnp.dot(mix_in[half], back_in[half, ch], preferred_element_type=F32)
            part_out[half, ch] = parts.astype(BF16)
            for q in FAR_FIRST:
                part_copy(ch)(half, q).start()
    for ch in range(2):
        for half in range(2):
            lanes = slice(half * HALF + ch * PART, half * HALF + (ch + 1) * PART)
            total = residual[:, lanes] + part_out[half, ch, 0:ROWS].astype(F32)
            for q in range(1, RING):
                arrived(part_copy(ch), half, q)
                total = total + part_in[half, ch, q * ROWS : (q + 1) * ROWS].astype(F32)
            for t in range(STEPS):
                out[:, t, lanes] = total[t * S_DEV : (t + 1) * S_DEV].astype(BF16)

    for half in range(2):
        for q in range(1, RING):
            info_copy(half, q).wait_send()
            for i in range(2):
                for copy_of in (row_copy, slot_copy, back_copy, part_copy):
                    copy_of(i)(half, q).wait_send()
    for q, core in pairs:
        there = peer(q, core)
        copy_aux(there, me).wait_send()
        for u in range(2):
            copy_px(u, there, me).wait_send()
            copy_reads(u, there, me).wait_send()


def per_device(
    prompt_state,
    prompt_conv,
    slot_prompt,
    projected,
    conv_weight,
    log_decay,
    write_rate,
    gate_in,
    layer_in,
    head_gain,
    post_gain,
    expert_ids,
    route_weight,
    w_gate_up,
    w_down,
):
    vmem = pl.BlockSpec(memory_space=pltpu.VMEM)
    hbm = pl.BlockSpec(memory_space=pl.ANY)
    dma = pltpu.SemaphoreType.DMA

    return pl.pallas_call(
        layer_kernel,
        out_shape=jax.ShapeDtypeStruct(layer_in.shape, BF16),
        in_specs=[vmem] * 13 + [hbm] * 2,
        out_specs=vmem,
        scratch_shapes=[
            pltpu.VMEM((D, 2 * FE), BF16),
            pltpu.VMEM((FE, D), BF16),
            pltpu.VMEM((2, HEADS, 16, CH), BF16),
            pltpu.VMEM((HEADS, S_DEV, 128), F32),
            pltpu.VMEM((2, HEADS, 16, CH), BF16),
            pltpu.VMEM((HEADS, S_DEV, 128), F32),
            pltpu.VMEM((DK, PG * DK), BF16),
            pltpu.VMEM((HEADS, 4, S_DEV, DK), F32),
            pltpu.VMEM((2, HEADS, 16, DK), BF16),
            pltpu.VMEM((2, HEADS, 16, DK), BF16),
            pltpu.VMEM((ROWS, D), F32),
            pltpu.VMEM((ROWS, D), F32),
            pltpu.VMEM((2, ROWS, HALF), BF16),
            pltpu.VMEM((2, RING, RING, 128), F32),
            pltpu.VMEM((2, RING, RING, 128), F32),
            pltpu.VMEM((2, RING * ROWS, HALF), BF16),
            pltpu.VMEM((2, 512, RING * ROWS), BF16),
            pltpu.VMEM((2, RING * ROWS, 512), BF16),
            pltpu.VMEM((2, 2, 512, PART), BF16),
            pltpu.VMEM((2, 2, 512, PART), BF16),
            pltpu.VMEM((2, 512, 2 * FE), F32),
            pltpu.VMEM((2, 512, FE), F32),
            pltpu.VMEM((2, 2, 512, PART), BF16),
            pltpu.VMEM((2, 2, 512, PART), BF16),
            pltpu.VMEM((2, 2, RING * ROWS, PART), BF16),
            pltpu.VMEM((2, 2, RING * ROWS, PART), BF16),
            dma((2,)),
            dma((5, HEADS)),
            dma((5, HEADS)),
            dma((18, RING)),
            dma((18, RING)),
        ],
        compiler_params=pltpu.CompilerParams(
            collective_id=0, has_side_effects=True, vmem_limit_bytes=VMEM_BYTES
        ),
        name="layer",
    )(
        projected,
        slot_prompt,
        log_decay,
        write_rate,
        prompt_state.reshape(PG, DK, DK),
        jnp.transpose(prompt_conv, (1, 2, 0, 3)).reshape(CONV - 1, PG, CH),
        conv_weight,
        head_gain.reshape(1, DK),
        gate_in,
        layer_in,
        post_gain.reshape(1, D),
        expert_ids,
        route_weight,
        w_gate_up.reshape(D, 2 * FE),
        w_down.reshape(FE, D),
    )


def solution(mesh):
    rows = ("rep", "exp")
    in_specs = (
        P("exp", "rep", None, None),
        P("exp", "rep", None, None),
        P(rows),
        P(rows, None, None, None),
        P(),
        P(rows, None, None),
        P(rows, None, None),
        P(rows, None, None),
        P(rows, None, None),
        P(),
        P(),
        P(rows, None, None),
        P(rows, None, None),
        P("exp", None, None),
        P("exp", None, None),
    )
    return jax.shard_map(
        per_device, mesh=mesh, in_specs=in_specs, out_specs=P(rows, None, None), check_vma=False
    )
```

time: 233 us -> 128 us (0.55)
  the two profiles are of different devices: /device:TPU:48 before, /device:TPU:1 now
where the time goes in v2:
time: 128 us; the launch traced here: 127 us
  Pallas kernels  126 us (98%)
  local copies, waits for them, and re-layouts  1.61 us (1%)
    pallas_call x1, Pallas kernels, per_device(): pl.pallas_call(layer_kernel, out_shape=jax.ShapeDtypeStruct(layer_in.shap...  126 us

profile of v2, /device:TPU:1, one launch (start us, length us, event | category | flops | bytes accessed | tf_op | source)
XLA Modules:
  0.0 127.3 jit_solution(7887481275089261445)
XLA Ops:
  0.0 125.7 %layer.1 = bf16[8,4,2048]{2,1,0:T(4,128)(2,1)} custom-call(bf16[8,4,16,384]{3,2,1,0:T(8,128)(2,1)} %projected_in.1, s32[8]{0:T(128)} %slot_prompt.1, f32[8,4,16]{2,1,0:T(4,128)} %log_decay.1, f32[8,4,16]{2,1,0:T(4,128)} %write_rate.1, bf16[8,128,128]{2,1,0:T(8,128)(2,1)} %bitcast.10, bf16[3,8,384]{2,1,0:T(8,128)(2,1)} %bitcast.11, bf16[16,4,384]{2,1,0:T(4,128)(2,1)} %taps.1, ...), custom_call_target="tpu_custom_call" | custom-call | tf_op jit(solution)/shard_map/layer/pallas_call | solution.py:521
  125.7 1.6 %copy.17 = bf16[8,4,2048]{2,1,0:T(4,128)(2,1)} copy(bf16[8,4,2048]{2,1,0:T(4,128)(2,1)} %layer.1) | data formatting | bytes 262144

commit v3 on v2

--- a/solution.py
+++ b/solution.py
@@ -51,12 +51,12 @@
     slot_prompt,
     log_decay,
     write_rate,
-    state,
+    state_hbm,
     conv,
     taps,
     head_gain,
-    gate_in,
-    layer_in,
+    gate_hbm,
+    layer_hbm,
     post_gain,
     ids,
     route,
@@ -65,6 +65,9 @@
     out,
     gate_up,
     down,
+    state,
+    gate_in,
+    layer_in,
     px,
     aux,
     got_px,
@@ -101,6 +104,10 @@
 
     load_gate_up = pltpu.make_async_copy(gate_up_hbm, gate_up, load_sem.at[0])
     load_down = pltpu.make_async_copy(down_hbm, down, load_sem.at[1])
+    load_inputs = [
+        pltpu.make_async_copy(src, dst, load_sem.at[2 + i])
+        for i, (src, dst) in enumerate(((state_hbm, state), (gate_hbm, gate_in), (layer_hbm, layer_in)))
+    ]
 
     def peer(q, core):
         odd = lax.rem(q, 2)
@@ -122,6 +129,8 @@
     for q in FAR_FIRST:
         for axis in (along_y, along_z):
             pl.semaphore_signal(barrier, inc=1, device_id=axis(OFFS[q]), device_id_type=MESH)
+    for load in load_inputs:
+        load.start()
     load_gate_up.start()
     load_down.start()
 
@@ -155,19 +164,23 @@
         turned = scalars if h == 0 else pltpu.roll(scalars, 128 - h, 1)
         aux[h] = jnp.where(tile_lane == 1, slot_column, turned)
 
-    for u in range(2):
+    def lay_out(u):
         turned = [jnp.swapaxes(projected_in[:, 2 * u + i].astype(F32), 0, 1) for i in range(2)]
         px[u] = jnp.concatenate(turned, axis=1).astype(BF16)
 
+    lay_out(0)
     pl.semaphore_wait(barrier, len(pairs) + 2 * (RING - 1))
     for q, core in pairs:
         there = peer(q, core)
         copy_aux(there, me).start()
         copy_px(0, there, me).start()
 
+    lay_out(1)
     got_aux[pl.ds(me, 1)] = aux[pl.ds(me, 1)]
     for u in range(2):
         got_px[u, pl.ds(me, 1)] = px[u, pl.ds(me, 1)]
+    for load in load_inputs:
+        load.wait()
     for p in range(PG):
         states[:, p * DK : (p + 1) * DK] = state[p]
     for t in range(STEPS):
@@ -316,35 +329,38 @@
                 kept[src, i] = value
         return jnp.concatenate(outs, axis=0).astype(BF16)
 
-    def heads_step(u):
-        def step(q, carry):
-            first = peer(q, 0)
-            second = peer(q, 1)
-
-            @pl.when(q > 0)
-            def _():
+    def heads_step(u, count):
+        def step(i, carry):
+            at = [(RING - 1 - i * count - j, core) for j in range(count) for core in range(2)]
+            sources = [peer(q, core) for q, core in at]
+
+            def each_other(act):
+                for (q, core), src in zip(at, sources):
+                    if core:
+                        act(src)
+                    else:
+
+                        @pl.when(q > 0)
+                        def _(src=src):
+                            act(src)
+
+            def wait(src):
                 if u == 0:
-                    copy_aux(first, first).wait_recv()
-                copy_px(u, first, first).wait_recv()
-
+                    copy_aux(src, src).wait_recv()
+                copy_px(u, src, src).wait_recv()
+
+            def send(src):
+                copy_reads(u, src, me).start()
+
+            each_other(wait)
             if u == 0:
-                copy_aux(second, second).wait_recv()
-            copy_px(u, second, second).wait_recv()
-            parts = [features(u, first), features(u, second)]
+                each_other(lambda src: copy_px(1, src, me).start())
+            parts = [features(u, src) for src in sources]
             stacked = jnp.concatenate([v for part in parts for v in part[1] + part[2]], axis=0).astype(BF16)
             projected = jnp.dot(stacked, states[...], preferred_element_type=F32)
-            for i, src in enumerate((first, second)):
-                reads[u, pl.ds(src, 1)] = recur(u, src, *parts[i], projected[i * 32 : (i + 1) * 32])[None]
-
-            @pl.when(q > 0)
-            def _():
-                copy_reads(u, first, me).start()
-                if u == 0:
-                    copy_px(1, first, me).start()
-
-            copy_reads(u, second, me).start()
-            if u == 0:
-                copy_px(1, second, me).start()
+            for k, src in enumerate(sources):
+                reads[u, pl.ds(src, 1)] = recur(u, src, *parts[k], projected[k * 32 : (k + 1) * 32])[None]
+            each_other(send)
             return carry
 
         return step
@@ -371,10 +387,10 @@
             for half in range(2):
                 row_copy(u)(half, q).start()
 
-    lax.fori_loop(0, RING, heads_step(0), 0)
-    lax.fori_loop(0, RING // 2, heads_step(1), 0)
+    lax.fori_loop(0, RING // 2, heads_step(0, 2), 0)
+    lax.fori_loop(0, RING // 4, heads_step(1, 2), 0)
     mix(0)
-    lax.fori_loop(RING // 2, RING, heads_step(1), 0)
+    lax.fori_loop(RING // 4, RING // 2, heads_step(1, 2), 0)
 
     cols = RING * ROWS
     earlier = (
@@ -521,11 +537,14 @@
     return pl.pallas_call(
         layer_kernel,
         out_shape=jax.ShapeDtypeStruct(layer_in.shape, BF16),
-        in_specs=[vmem] * 13 + [hbm] * 2,
+        in_specs=[vmem] * 4 + [hbm] + [vmem] * 3 + [hbm] * 2 + [vmem] * 3 + [hbm] * 2,
         out_specs=vmem,
         scratch_shapes=[
             pltpu.VMEM((D, 2 * FE), BF16),
             pltpu.VMEM((FE, D), BF16),
+            pltpu.VMEM((PG, DK, DK), BF16),
+            pltpu.VMEM((S_DEV, STEPS, D), BF16),
+            pltpu.VMEM((S_DEV, STEPS, D), BF16),
             pltpu.VMEM((2, HEADS, 16, CH), BF16),
             pltpu.VMEM((HEADS, S_DEV, 128), F32),
             pltpu.VMEM((2, HEADS, 16, CH), BF16),
@@ -550,7 +569,7 @@
             pltpu.VMEM((2, 2, 512, PART), BF16),
             pltpu.VMEM((2, 2, RING * ROWS, PART), BF16),
             pltpu.VMEM((2, 2, RING * ROWS, PART), BF16),
-            dma((2,)),
+            dma((5,)),
             dma((5, HEADS)),
             dma((5, HEADS)),
             dma((18, RING)),

time: 128 us -> 125 us (0.977)
  Pallas kernels: 126 us -> 124 us
    pallas_call x1, Pallas kernels: 126 us -> 124 us  [per_device(): pl.pallas_call(layer_kernel, out_shape=jax.ShapeDtypeStruct(layer_in.shap...]
where the time goes in v3:
time: 125 us
  Pallas kernels  124 us (99%)
  local copies, waits for them, and re-layouts  1.61 us (1%)
    pallas_call x1, Pallas kernels, per_device(): pl.pallas_call(layer_kernel, out_shape=jax.ShapeDtypeStruct(layer_in.shap...  124 us

profile of v3, /device:TPU:1, one launch (start us, length us, event | category | flops | bytes accessed | tf_op | source)
XLA Modules:
  0.0 125.1 jit_solution(12023952154098311445)
XLA Ops:
  0.0 123.5 %layer.1 = bf16[8,4,2048]{2,1,0:T(4,128)(2,1)} custom-call(bf16[8,4,16,384]{3,2,1,0:T(8,128)(2,1)} %projected_in.1, s32[8]{0:T(128)} %slot_prompt.1, f32[8,4,16]{2,1,0:T(4,128)} %log_decay.1, f32[8,4,16]{2,1,0:T(4,128)} %write_rate.1, bf16[8,128,128]{2,1,0:T(8,128)(2,1)} %bitcast.10, bf16[3,8,384]{2,1,0:T(8,128)(2,1)} %bitcast.11, bf16[16,4,384]{2,1,0:T(4,128)(2,1)} %taps.1, ...), custom_call_target="tpu_custom_call" | custom-call | tf_op jit(solution)/shard_map/layer/pallas_call | solution.py:537
  123.5 1.6 %copy.17 = bf16[8,4,2048]{2,1,0:T(4,128)(2,1)} copy(bf16[8,4,2048]{2,1,0:T(4,128)(2,1)} %layer.1) | data formatting | bytes 262144
